TPU v7x, 32 devices: a whole 2x2x4 slice. The times are simulated.
32 devices in a mesh: gx: 8 (over z, y), gy: 4 (over x, core).
Axes of the slice: x: 2, y: 2, z: 4, core: 2. Of those that a mesh axis runs over, the one named last changes fastest.
Arguments:
- positions: float32 [3, 8, 4, 512], P(None, 'gx', 'gy'), may hold values from -0.1 to 255.6, as said below
- species: int32 [8, 4, 512], P('gx', 'gy'), may hold values 0 or 1
- counts: int32 [8, 4], P('gx', 'gy'), may hold values from 16 to 512, as said below
- neighbours: int32 [64, 8, 4, 512], P(None, 'gx', 'gy'), may hold values from 4 to 140, as said below
- embed_weight: bfloat16 [64, 12], replicated, may hold values from -1.75 to 1.75
- mixer_weight: bfloat16 [64, 64], replicated, may hold values from -0.75 to 0.75
- tensor_weight: bfloat16 [32, 64], replicated, may hold values from -0.75 to 0.75
- update_weight: bfloat16 [64, 96], replicated, may hold values from -0.625 to 0.625
- output_weight: float32 [64], replicated, may hold values from -0.75 to 0.75
- pair_scale: float32 [2, 2], replicated, may hold values from 0.1 to 1.9
Outputs:
- atom_energy: float32 [8, 4, 512], P('gx', 'gy')
- forces: float32 [3, 8, 4, 512], P(None, 'gx', 'gy')
Inputs may be any that keep to these rules, and one draw needn't show every extreme that they name: `counts`: at least one column holds 512 atoms. `neighbours`: o runs 0..8; t runs -8..7 for the own column (o = 4), -6..6 for the four side columns (o odd), -4..4 for the four diagonal ones; one atom's entries are distinct and never (o, t) = (4, 0). `positions`: x and y lie 0.45 to 4.05 from the corner of a column 4.5 wide; the height of slot s lies within 0.1 of s / 2.
All inputs are finite; a program needn't handle non-finite values. No bound on the sum of `species` on one device may be relied on, other than what follows from the above.
Results may differ from a plain program's by a relative error of at most 0.014.
Values sent between devices are 32-bit elements; how exact they have to be, the bound alone decides.
A program may use at most 128 MiB of HBM per device.

v0:
```python
import math

import jax
import jax.numpy as jnp
from jax import lax
from jax.experimental import pallas as pl
from jax.experimental.pallas import tpu as pltpu
from jax.sharding import PartitionSpec as P

cutoff = 4.5
col_width = 4.5
root_three = math.sqrt(3.0)
LANES = 128
ROWS = 8
REACH = 8
STRIDES = 16
VMEM_LIMIT = 48 * 1024 * 1024
F32 = jnp.float32
BF16 = jnp.bfloat16


def mm(a, b):
    return jnp.dot(a, b, preferred_element_type=F32)


def wrapped_index(shape, axis, count):
    wide = lax.broadcasted_iota(jnp.int32, shape, axis).astype(F32) - REACH
    turns = jnp.floor((wide + 0.5) / count)
    return wide - turns * count


def split(value, terms):
    pieces = []
    for _ in range(terms):
        piece = value.astype(BF16)
        pieces.append(piece)
        value = value - piece.astype(F32)
    return pieces


def spread_kernel(count_ref, column_ref, wide_ref):
    rows, slots = column_ref.shape
    width = wide_ref.shape[1]
    count = count_ref[0, 0].astype(F32)
    hot = (
        wrapped_index((slots, width), 1, count)
        == lax.broadcasted_iota(jnp.int32, (slots, width), 0).astype(F32)
    )
    table = jnp.where(hot, 1.0, 0.0).astype(BF16)
    high, middle, low = split(column_ref[...], 3)
    wide_ref[...] = (mm(low, table) + mm(middle, table)) + mm(high, table)


def fold_kernel(count_ref, wide_ref, out_ref):
    width = wide_ref.shape[1]
    slots = out_ref.shape[1]
    count = count_ref[0, 0].astype(F32)
    hot = (
        wrapped_index((width, slots), 0, count)
        == lax.broadcasted_iota(jnp.int32, (width, slots), 1).astype(F32)
    )
    table = jnp.where(hot, 1.0, 0.0).astype(BF16)
    high, middle, low = split(wide_ref[...], 3)
    out_ref[...] = (mm(low, table) + mm(middle, table)) + mm(high, table)


def codes_of(index):
    reach = lambda o: 8 if o == 4 else (6 if o % 2 else 4)
    return [o for o in range(9) if abs(index - 8) <= reach(o) and (o, index) != (4, 8)]


def row_of(tile):
    return jnp.concatenate([tile[i : i + 1, :] for i in range(ROWS)], axis=1)


def tile_of(row):
    return jnp.concatenate([row[:, i * LANES : (i + 1) * LANES] for i in range(ROWS)], axis=0)


def lane_sum(value):
    parts = [value[:, i * LANES : (i + 1) * LANES] for i in range(ROWS)]
    while len(parts) > 1:
        parts = [parts[i] + parts[i + 1] for i in range(0, len(parts), 2)]
    return parts[0]


def repeat(value):
    return jnp.concatenate([value] * ROWS, axis=1)


def column_sum(value):
    return jnp.sum(value, axis=0, keepdims=True)


def silu_pair(x):
    sig = 0.5 * jnp.tanh(0.5 * x) + 0.5
    s = x * sig
    return s, sig + s - s * sig


SIN = [(-1) ** i * math.pi ** (2 * i + 1) / math.factorial(2 * i + 1) for i in range(6)]
COS = [(-1) ** i * math.pi ** (2 * i) / math.factorial(2 * i) for i in range(7)]


def poly(x, coefficients):
    total = jnp.full_like(x, coefficients[-1])
    for c in coefficients[-2::-1]:
        total = total * x + c
    return total


DIST, INV, ENV, WEIGHT, SCALE, HX, HY, HZ, OTHER = range(9)
D_ENV, D_DIST, D_HX, D_HY, D_HZ = range(5)


def layer_kernel(
    count_ref,
    scale_ref,
    table_ref,
    own_ref,
    codes_ref,
    embed_ref,
    mixer_ref,
    tensor_ref,
    update_ref,
    embed_t_ref,
    mixer_t_ref,
    tensor_t_ref,
    update_t_ref,
    output_ref,
    energy_ref,
    wide_ref,
    plane,
    dplane,
    bessel_d,
    hidden_d,
    latent,
    mixed,
    mixed_d,
    tensor,
    latent_g,
    feature_g,
    environment,
    environment_g,
    per_stride,
):
    block = pl.program_id(0)
    neigh = codes_ref.shape[0]
    chunks = neigh // ROWS
    span = ROWS * LANES
    width = 2 * LANES

    @pl.when(block == 0)
    def _():
        wide_ref[...] = jnp.zeros_like(wide_ref)
        per_stride[...] = jnp.zeros_like(per_stride)

    start = pl.multiple_of(block * LANES, LANES)
    slab = table_ref[:, pl.ds(start, width)]
    codes = codes_ref[...]

    found = [jnp.zeros((neigh, LANES), F32) for _ in range(4)]
    for index in range(STRIDES):
        turned = slab if index == 0 else pltpu.roll(slab, width - index, 1)
        for o in codes_of(index):
            here = codes == STRIDES * o + index
            for a in range(4):
                row = turned[4 * o + a : 4 * o + a + 1, :LANES]
                found[a] = jnp.where(here, row, found[a])
    own = own_ref[...]
    dx, dy, dz = (found[a] - own[a : a + 1, :] for a in range(3))
    other = found[3]
    kind = own[3:4, :]
    slot = lax.broadcasted_iota(jnp.int32, (1, LANES), 1) + start
    live = jnp.where(slot < count_ref[0, 0], 1.0, 0.0)
    square = dx * dx + dy * dy + dz * dz
    inverse = lax.rsqrt(square)
    distance = square * inverse
    x = distance / cutoff
    x2 = x * x
    x5 = x2 * x2 * x
    x6 = x5 * x
    inside = x < 1.0
    env = jnp.where(inside, 1.0 + x6 * (-28.0 + x * (48.0 - 21.0 * x)), 0.0)
    env_slope = jnp.where(inside, x5 * (-168.0 + x * (336.0 - 168.0 * x)) / cutoff, 0.0)
    scale = live * (
        (1.0 - kind) * (scale_ref[0, 0] * (1.0 - other) + scale_ref[0, 1] * other)
        + kind * (scale_ref[1, 0] * (1.0 - other) + scale_ref[1, 1] * other)
    )
    reach3 = root_three * inverse
    plane[DIST] = jnp.minimum(distance, cutoff)
    plane[INV] = inverse
    plane[ENV] = env
    plane[WEIGHT] = env * scale
    plane[SCALE] = scale
    plane[HX] = dx * reach3
    plane[HY] = dy * reach3
    plane[HZ] = dz * reach3
    plane[OTHER] = other
    environment[...] = jnp.zeros_like(environment)
    environment_g[...] = jnp.zeros_like(environment_g)
    energy_ref[...] = jnp.zeros_like(energy_ref)

    def row(which, c):
        return row_of(plane[which, pl.ds(pl.multiple_of(c * ROWS, ROWS), ROWS), :])

    def put(which, c, value):
        dplane[which, pl.ds(pl.multiple_of(c * ROWS, ROWS), ROWS), :] = tile_of(value)

    order = lax.broadcasted_iota(jnp.int32, (8, span), 0)
    order_f = (order + 1).astype(F32)
    kind_row = repeat(kind)
    norm = math.sqrt(2.0 / cutoff)

    def first(c, carry):
        far, inv, envelope, partner = row(DIST, c), row(INV, c), row(ENV, c), row(OTHER, c)
        turns = order_f * (far * (1.0 / cutoff))
        whole = jnp.floor(turns + 0.5)
        part = turns - whole
        sign = 1.0 - 2.0 * (whole - 2.0 * jnp.floor(0.5 * whole))
        part2 = part * part
        scaled = sign * (norm * inv)
        bessel = scaled * (part * poly(part2, SIN))
        slope = scaled * poly(part2, COS)
        bessel_d[c] = (math.pi / cutoff) * order_f * slope - bessel * inv
        one_hot = jnp.where(
            order == 0,
            1.0 - kind_row,
            jnp.where(
                order == 1,
                kind_row,
                jnp.where(order == 2, 1.0 - partner, jnp.where(order == 3, partner, 0.0)),
            ),
        )
        inputs = jnp.concatenate([bessel, one_hot], axis=0).astype(BF16)
        hidden, slope_h = silu_pair(mm(embed_ref[...], inputs))
        hidden_d[c] = slope_h.astype(BF16)
        active, slope_m = silu_pair(mm(mixer_ref[...], hidden.astype(BF16)))
        mixed[c] = active.astype(BF16)
        mixed_d[c] = (slope_m * envelope).astype(BF16)
        lat = (active * envelope).astype(BF16)
        latent[c] = lat
        t = mm(tensor_ref[...], lat)
        tensor[c] = t
        env_w = t[:16]
        environment[0] += lane_sum(env_w)
        for m, which in enumerate((HX, HY, HZ)):
            environment[m + 1] += lane_sum(env_w * row(which, c))
        return carry

    lax.fori_loop(0, chunks, first, 0)

    def second(c, carry):
        weight = row(WEIGHT, c)
        harm = [row(which, c) for which in (HX, HY, HZ)]
        feat = tensor[c, 16:]
        envs = [repeat(environment[m]) for m in range(4)]
        mixed_env = harm[0] * envs[1] + harm[1] * envs[2] + harm[2] * envs[3]
        lat = latent[c]
        quarter = 0.25 * feat
        scalars = jnp.concatenate([quarter * envs[0], quarter * mixed_env], axis=0).astype(BF16)
        joined = jnp.concatenate([lat, scalars], axis=0)
        s, slope = silu_pair(mm(update_ref[...], joined))
        out = output_ref[...]
        value = column_sum(out * (lat.astype(F32) + s))
        energy_ref[...] += lane_sum(value * weight)
        put(D_ENV, c, value * row(SCALE, c))
        seed = out * weight
        back = mm(update_t_ref[...], (seed * slope).astype(BF16))
        latent_g[c] = (seed + back[:64]).astype(BF16)
        even_g, odd_g = 0.25 * back[64:80], 0.25 * back[80:96]
        feature_g[c] = (even_g * envs[0] + odd_g * mixed_env).astype(BF16)
        environment_g[0] += lane_sum(even_g * feat)
        odd = odd_g * feat
        for m in range(3):
            environment_g[m + 1] += lane_sum(odd * harm[m])
            put(D_HX + m, c, column_sum(odd * envs[m + 1]))
        return carry

    lax.fori_loop(0, chunks, second, 0)

    def third(c, carry):
        harm = [row(which, c) for which in (HX, HY, HZ)]
        grads = [repeat(environment_g[m]) for m in range(4)]
        env_w = tensor[c, :16]
        env_w_g = grads[0] + harm[0] * grads[1] + harm[1] * grads[2] + harm[2] * grads[3]
        tensor_g = jnp.concatenate([env_w_g.astype(BF16), feature_g[c]], axis=0)
        total = latent_g[c].astype(F32) + mm(tensor_t_ref[...], tensor_g)
        at = pl.ds(pl.multiple_of(c * ROWS, ROWS), ROWS)
        dplane[D_ENV, at, :] += tile_of(column_sum(total * mixed[c].astype(F32)))
        mixed_g = (total * mixed_d[c].astype(F32)).astype(BF16)
        hidden_g = mm(mixer_t_ref[...], mixed_g)
        hidden_g = (hidden_g * hidden_d[c].astype(F32)).astype(BF16)
        bessel_g = mm(embed_t_ref[...], hidden_g)[:8]
        put(D_DIST, c, column_sum(bessel_g * bessel_d[c]))
        for m in range(3):
            dplane[D_HX + m, at, :] += tile_of(column_sum(env_w * grads[m + 1]))
        return carry

    lax.fori_loop(0, chunks, third, 0)

    hx, hy, hz = plane[HX], plane[HY], plane[HZ]
    gx, gy, gz = dplane[D_HX], dplane[D_HY], dplane[D_HZ]
    inverse = plane[INV]
    slope = dplane[D_DIST] + dplane[D_ENV] * env_slope
    along = (slope - inverse * (hx * gx + hy * gy + hz * gz)) * (1.0 / root_three)
    side = root_three * inverse
    gradient = [side * gx + along * hx, side * gy + along * hy, side * gz + along * hz]

    for index in range(STRIDES):
        for o in codes_of(index):
            here = codes == STRIDES * o + index
            for a in range(3):
                at = 3 * o + a
                per_stride[index, at : at + 1, :] = -column_sum(jnp.where(here, gradient[a], 0.0))
    for a in range(3):
        per_stride[8, 12 + a : 13 + a, :] = column_sum(gradient[a])
    lines = per_stride.shape[1]
    total = jnp.zeros((lines, width), F32)
    for index in range(STRIDES):
        laid = jnp.concatenate([per_stride[index], jnp.zeros((lines, LANES), F32)], axis=1)
        total = total + (laid if index == 0 else pltpu.roll(laid, index, 1))
    wide_ref[:, pl.ds(start, width)] += total


def shifted(value, axis, by):
    peers = lax.axis_size(axis)
    return lax.ppermute(value, axis, [(i, (i + by) % peers) for i in range(peers)])


def body(
    positions,
    species,
    counts,
    neighbours,
    embed_weight,
    mixer_weight,
    tensor_weight,
    update_weight,
    output_weight,
    pair_scale,
):
    slots = positions.shape[3]
    neigh = neighbours.shape[0]
    width = slots + LANES
    vmem = pl.BlockSpec(memory_space=pltpu.VMEM)
    smem = pl.BlockSpec(memory_space=pltpu.SMEM)
    params = pltpu.CompilerParams(vmem_limit_bytes=VMEM_LIMIT)
    column = jnp.concatenate(
        [positions.reshape(3, slots), species.reshape(1, slots).astype(F32)], axis=0
    )
    wide = pl.pallas_call(
        spread_kernel,
        out_shape=jax.ShapeDtypeStruct((4, width), F32),
        in_specs=[smem, vmem],
        out_specs=vmem,
        compiler_params=params,
    )(counts, column)
    beside = jnp.stack([shifted(wide, "gx", 1), wide, shifted(wide, "gx", -1)])
    around = jnp.stack([shifted(beside, "gy", 1), beside, shifted(beside, "gy", -1)], axis=1)
    steps = jnp.arange(3, dtype=F32) - 1.0
    shift = jnp.stack(
        [
            jnp.broadcast_to(col_width * steps[:, None], (3, 3)),
            jnp.broadcast_to(col_width * steps[None, :], (3, 3)),
            jnp.zeros((3, 3), F32),
            jnp.zeros((3, 3), F32),
        ],
        axis=2,
    )
    table = (around + shift[..., None]).reshape(36, width)

    chunks = neigh // ROWS
    span = ROWS * LANES
    latent = mixer_weight.shape[0]
    embed = jnp.pad(embed_weight, ((0, 0), (0, 4)))
    whole = lambda array: pl.BlockSpec(array.shape, lambda b: (0,) * array.ndim)
    by_block = lambda rows: pl.BlockSpec((rows, LANES), lambda b: (0, b))
    operands = [
        embed,
        mixer_weight,
        tensor_weight,
        update_weight,
        embed.T,
        mixer_weight.T,
        tensor_weight.T,
        update_weight.T,
        output_weight.reshape(latent, 1),
    ]
    energy, partials = pl.pallas_call(
        layer_kernel,
        grid=(slots // LANES,),
        out_shape=(
            jax.ShapeDtypeStruct((1, slots), F32),
            jax.ShapeDtypeStruct((27, width), F32),
        ),
        in_specs=[smem, smem, whole(table), by_block(4), by_block(neigh)]
        + [whole(array) for array in operands],
        out_specs=(by_block(1), pl.BlockSpec((27, width), lambda b: (0, 0))),
        scratch_shapes=[
            pltpu.VMEM((9, neigh, LANES), F32),
            pltpu.VMEM((5, neigh, LANES), F32),
            pltpu.VMEM((chunks, 8, span), F32),
            pltpu.VMEM((chunks, latent, span), BF16),
            pltpu.VMEM((chunks, latent, span), BF16),
            pltpu.VMEM((chunks, latent, span), BF16),
            pltpu.VMEM((chunks, latent, span), BF16),
            pltpu.VMEM((chunks, 32, span), F32),
            pltpu.VMEM((chunks, latent, span), BF16),
            pltpu.VMEM((chunks, 16, span), BF16),
            pltpu.VMEM((4, 16, LANES), F32),
            pltpu.VMEM((4, 16, LANES), F32),
            pltpu.VMEM((STRIDES, 27, LANES), F32),
        ],
        compiler_params=params,
    )(counts, pair_scale, table, column, neighbours.reshape(neigh, slots), *operands)

    partials = partials.reshape(3, 3, 3, width)
    line = partials[1] + shifted(partials[0], "gx", -1) + shifted(partials[2], "gx", 1)
    centre = line[1] + shifted(line[0], "gy", -1) + shifted(line[2], "gy", 1)
    forces = pl.pallas_call(
        fold_kernel,
        out_shape=jax.ShapeDtypeStruct((3, slots), F32),
        in_specs=[smem, vmem],
        out_specs=vmem,
        compiler_params=params,
    )(counts, centre)
    return energy.reshape(1, 1, slots), forces.reshape(3, 1, 1, slots)


def solution(mesh):
    return jax.shard_map(
        body,
        mesh=mesh,
        in_specs=(
            P(None, "gx", "gy", None),
            P("gx", "gy", None),
            P("gx", "gy"),
            P(None, "gx", "gy", None),
            P(),
            P(),
            P(),
            P(),
            P(),
            P(),
        ),
        out_specs=(P("gx", "gy", None), P(None, "gx", "gy", None)),
        check_vma=False,
    )
```

profile of v0, /device:TPU:0, one launch (start us, length us, event | category | flops | bytes accessed | tf_op | source)
XLA Modules:
  0.0 89.3 jit_solution(13566510456831346690)
XLA Ops:
  1.3 0.7 convert_bitcast_fusion
  2.0 0.7 copy.25
  2.7 0.4 shard_map.113
  3.1 6.0 %collective-permute-start.1 = (f32[4,640]{1,0:T(4,128)S(1)}, f32[4,640]{1,0:T(4,128)S(1)}, u32[]{:S(2)}, u32[]{:S(2)}) collective-permute-start(f32[4,640]{1,0:T(4,128)S(1)} %shard_map.113), channel_id=1, source_target_pairs={{0,28},{4,0},{8,4},{12,8},{16,12},{20,16},{24,20},{28,24},{1,29},{... | collective-permute-start | bytes 30728 | tf_op jit(solution)/shard_map/ppermute | solution.py:328
  9.1 0.1 pad.7.clone
  9.2 0.1 stack_broadcast_in_dim.5
  9.2 0.1 stack_broadcast_in_dim.4
  9.3 0.1 maximum_maximum_fusion
  9.4 1.1 %collective-permute-done.1 = f32[4,640]{1,0:T(4,128)S(1)} collective-permute-done((f32[4,640]{1,0:T(4,128)S(1)}, f32[4,640]{1,0:T(4,128)S(1)}, u32[]{:S(2)}, u32[]{:S(2)}) %collective-permute-start.1) | collective-permute-done | bytes 10272 | tf_op jit(solution)/shard_map/ppermute | solution.py:328
  10.5 5.0 %collective-permute-done = f32[4,640]{1,0:T(4,128)S(1)} collective-permute-done((f32[4,640]{1,0:T(4,128)S(1)}, f32[4,640]{1,0:T(4,128)S(1)}, u32[]{:S(2)}, u32[]{:S(2)}) %collective-permute-start) | collective-permute-done | bytes 10272 | tf_op jit(solution)/shard_map/ppermute | solution.py:328
  15.5 0.5 collective-permute-start.2
  16.0 0.1 copy.23
  16.2 0.1 add.33
  16.3 0.1 copy.13
  16.4 0.6 copy-done.2
  17.0 0.1 copy.14
  17.0 0.6 copy-done.1
  17.7 0.1 copy.15
  17.8 0.7 copy-done.6
  18.4 0.1 copy.17.output_ref
  18.6 0.6 collective-permute-done.2
  19.3 0.1 broadcast_add_fusion.table_ref
  19.4 0.7 copy-done.3
  20.1 58.2 %shard_map.114 = (f32[1,512]{1,0:T(1,128)}, f32[27,640]{1,0:T(8,128)S(1)}) custom-call(s32[1,1]{1,0:T(1,128)S(6)} %copy.26.count_ref, f32[2,2]{1,0:T(2,128)S(1)} %copy-done.3, f32[36,640]{1,0:T(8,128)S(1)} %broadcast_add_fusion.table_ref, f32[4,512]{1,0:T(4,128)S(1)} %pad_maximum_fusion.2.column_ref.own_ref, s32[64,512]{1,0:T(8,128)S(1)} %bitcast.33, ...), custom_call_target="tpu_custom_call" | custom-call | tf_op jit(solution)/shard_map/pallas_call | solution.py:390
  78.3 0.1 collective-permute-start.5
  78.4 4.7 %collective-permute-start.4 = (f32[3,3,640]{2,1,0:T(4,128)S(1)}, f32[3,3,640]{2,1,0:T(4,128)S(1)}, u32[]{:S(2)}, u32[]{:S(2)}) collective-permute-start(f32[3,3,640]{2,1,0:T(4,128)S(1)} %squeeze.19), channel_id=1, source_target_pairs={{0,28},{4,0},{8,4},{12,8},{16,12},{20,16},{24,20},{28,24},{1,29},{... | collective-permute-start | bytes 69128 | tf_op jit(solution)/shard_map/ppermute | solution.py:328
  83.1 1.9 %collective-permute-done.5 = f32[3,3,640]{2,1,0:T(4,128)S(1)} collective-permute-done((f32[3,3,640]{2,1,0:T(4,128)S(1)}, f32[3,3,640]{2,1,0:T(4,128)S(1)}, u32[]{:S(2)}, u32[]{:S(2)}) %collective-permute-start.5) | collective-permute-done | bytes 23072 | tf_op jit(solution)/shard_map/ppermute | solution.py:328
  85.1 0.5 collective-permute-start.7
  85.6 0.9 collective-permute-done.6
  86.4 1.8 %collective-permute-done.7 = f32[3,640]{1,0:T(4,128)S(1)} collective-permute-done((f32[3,640]{1,0:T(4,128)S(1)}, f32[3,640]{1,0:T(4,128)S(1)}, u32[]{:S(2)}, u32[]{:S(2)}) %collective-permute-start.7) | collective-permute-done | bytes 7712 | tf_op jit(solution)/shard_map/ppermute | solution.py:328
  88.2 0.5 shard_map.115
  88.7 0.6 copy.18
  (32 shorter events, 0.3 us)
Async XLA Ops:
  3.1 7.4 %collective-permute-start.1 = (f32[4,640]{1,0:T(4,128)S(1)}, f32[4,640]{1,0:T(4,128)S(1)}, u32[]{:S(2)}, u32[]{:S(2)}) collective-permute-start(f32[4,640]{1,0:T(4,128)S(1)} %shard_map.113), channel_id=1, source_target_pairs={{0,28},{4,0},{8,4},{12,8},{16,12},{20,16},{24,20},{28,24},{1,29},{... | collective-permute-start | bytes 30728 | tf_op jit(solution)/shard_map/ppermute | solution.py:328
  9.1 6.4 %collective-permute-start = (f32[4,640]{1,0:T(4,128)S(1)}, f32[4,640]{1,0:T(4,128)S(1)}, u32[]{:S(2)}, u32[]{:S(2)}) collective-permute-start(f32[4,640]{1,0:T(4,128)S(1)} %shard_map.113), channel_id=1, source_target_pairs={{0,4},{4,8},{8,12},{12,16},{16,20},{20,24},{24,28},{28,0},{1,5},{5... | collective-permute-start | bytes 30728 | tf_op jit(solution)/shard_map/ppermute | solution.py:328
  9.2 6.8 %copy-start.5 = (bf16[64,12]{0,1:T(8,128)(2,1)S(1)}, bf16[64,12]{0,1:T(8,128)(2,1)}, u32[]{:S(2)}) copy-start(bf16[64,12]{0,1:T(8,128)(2,1)} %param.14) | copy-start | bytes 4612
  9.3 9.2 %copy-start.4 = (s32[64,1,1,512]{3,2,1,0:T(1,128)S(1)}, s32[64,1,1,512]{3,2,1,0:T(1,128)}, u32[]{:S(2)}) copy-start(s32[64,1,1,512]{3,2,1,0:T(1,128)} %param.13) | copy-start | bytes 393220
  15.5 0.8 copy-start
  15.5 3.1 %collective-permute-start.3 = (f32[3,4,640]{2,1,0:T(4,128)S(1)}, f32[3,4,640]{2,1,0:T(4,128)S(1)}, u32[]{:S(2)}, u32[]{:S(2)}) collective-permute-start(f32[3,4,640]{2,1,0:T(4,128)S(1)} %get-tuple-element.14), channel_id=1, source_target_pairs={{0,3},{1,0},{2,1},{3,2},{4,7},{5,4},{6,5},{7,6},{8,11},{9,8},{10,9... | collective-permute-start | bytes 92168 | tf_op jit(solution)/shard_map/ppermute | solution.py:328
  15.5 3.7 %collective-permute-start.2 = (f32[3,4,640]{2,1,0:T(4,128)S(1)}, f32[3,4,640]{2,1,0:T(4,128)S(1)}, u32[]{:S(2)}, u32[]{:S(2)}) collective-permute-start(f32[3,4,640]{2,1,0:T(4,128)S(1)} %get-tuple-element.14), channel_id=1, source_target_pairs={{0,1},{1,2},{2,3},{3,0},{4,5},{5,6},{6,7},{7,4},{8,9},{9,10},{10,1... | collective-permute-start | bytes 92168 | tf_op jit(solution)/shard_map/ppermute | solution.py:328
  16.2 0.7 copy-start.2
  16.9 0.7 copy-start.1
  17.8 0.7 copy-start.6
  19.4 0.7 copy-start.3
  78.3 6.6 %collective-permute-start.5 = (f32[3,3,640]{2,1,0:T(4,128)S(1)}, f32[3,3,640]{2,1,0:T(4,128)S(1)}, u32[]{:S(2)}, u32[]{:S(2)}) collective-permute-start(f32[3,3,640]{2,1,0:T(4,128)S(1)} %squeeze.20), channel_id=1, source_target_pairs={{0,4},{4,8},{8,12},{12,16},{16,20},{20,24},{24,28},{28,0},{1,5},{5... | collective-permute-start | bytes 69128 | tf_op jit(solution)/shard_map/ppermute | solution.py:328
  78.4 6.6 %collective-permute-start.4 = (f32[3,3,640]{2,1,0:T(4,128)S(1)}, f32[3,3,640]{2,1,0:T(4,128)S(1)}, u32[]{:S(2)}, u32[]{:S(2)}) collective-permute-start(f32[3,3,640]{2,1,0:T(4,128)S(1)} %squeeze.19), channel_id=1, source_target_pairs={{0,28},{4,0},{8,4},{12,8},{16,12},{20,16},{24,20},{28,24},{1,29},{... | collective-permute-start | bytes 69128 | tf_op jit(solution)/shard_map/ppermute | solution.py:328
  85.0 1.4 %collective-permute-start.6 = (f32[3,640]{1,0:T(4,128)S(1)}, f32[3,640]{1,0:T(4,128)S(1)}, u32[]{:S(2)}, u32[]{:S(2)}) collective-permute-start(f32[3,640]{1,0:T(4,128)S(1)} %get-tuple-element.11), channel_id=1, source_target_pairs={{0,3},{1,0},{2,1},{3,2},{4,7},{5,4},{6,5},{7,6},{8,11},{9,8},{10,9... | collective-permute-start | bytes 23048 | tf_op jit(solution)/shard_map/ppermute | solution.py:328
  85.1 3.1 %collective-permute-start.7 = (f32[3,640]{1,0:T(4,128)S(1)}, f32[3,640]{1,0:T(4,128)S(1)}, u32[]{:S(2)}, u32[]{:S(2)}) collective-permute-start(f32[3,640]{1,0:T(4,128)S(1)} %get-tuple-element.12), channel_id=1, source_target_pairs={{0,1},{1,2},{2,3},{3,0},{4,5},{5,6},{6,7},{7,4},{8,9},{9,10},{10,1... | collective-permute-start | bytes 23048 | tf_op jit(solution)/shard_map/ppermute | solution.py:328
where the time goes:
time: 89.7 us; the launch traced here: 89.3 us
  Pallas kernels  59.1 us (66%)
  starting transfers between devices  11.9 us (13%)
  waiting for transfers between devices  11.2 us (12%)
  local copies, waits for them, and re-layouts  4.8 us (5%)
  between operations  1.43 us (2%)
  other arithmetic  0.91 us (1%)
    pallas_call x1, Pallas kernels, body(): pl.pallas_call(layer_kernel, grid=(slots // LANES,), out_shape=(jax.Shape...  58.2 us
    ppermute x8, starting transfers between devices, shifted(): lax.ppermute(value, axis, [(i, (i + by) % peers) for i in range(peers)])  11.9 us
    ppermute x8, waiting for transfers between devices, shifted(): lax.ppermute(value, axis, [(i, (i + by) % peers) for i in range(peers)])  11.2 us
    unnamed x21, local copies, waits for them, and re-layouts  4.28 us
  transfers between devices with their start and end apart: 8, of which 6 were waited for; matrix products, arithmetic and copies ran while one was open for 1% of the time, Pallas kernels for 0%

commit v1 on v0

--- a/solution.py
+++ b/solution.py
@@ -38,30 +38,89 @@
     return pieces
 
 
-def spread_kernel(count_ref, column_ref, wide_ref):
+def beside(o):
+    gx, gy = lax.axis_size("gx"), lax.axis_size("gy")
+    return (
+        lax.rem(lax.axis_index("gx") + gx + (o // 3 - 1), gx),
+        lax.rem(lax.axis_index("gy") + gy + (o % 3 - 1), gy),
+    )
+
+
+AROUND = (3, 5, 1, 7, 0, 2, 6, 8)
+MESH = pl.DeviceIdType.MESH
+
+
+def greet():
+    for o in AROUND:
+        pl.semaphore_signal(
+            pltpu.get_barrier_semaphore(), inc=1, device_id=beside(o), device_id_type=MESH
+        )
+
+
+def to_column(o, source, held, send_sem, recv_sem):
+    return pltpu.make_async_remote_copy(
+        src_ref=source,
+        dst_ref=held.at[8 - o],
+        send_sem=send_sem.at[o],
+        recv_sem=recv_sem.at[8 - o],
+        device_id=beside(o),
+        device_id_type=MESH,
+    )
+
+
+def spread_kernel(count_ref, column_ref, table_ref, wide, held, send_sem, recv_sem):
+    greet()
     rows, slots = column_ref.shape
-    width = wide_ref.shape[1]
+    width = wide.shape[1]
     count = count_ref[0, 0].astype(F32)
     hot = (
         wrapped_index((slots, width), 1, count)
         == lax.broadcasted_iota(jnp.int32, (slots, width), 0).astype(F32)
     )
-    table = jnp.where(hot, 1.0, 0.0).astype(BF16)
+    hot = jnp.where(hot, 1.0, 0.0).astype(BF16)
     high, middle, low = split(column_ref[...], 3)
-    wide_ref[...] = (mm(low, table) + mm(middle, table)) + mm(high, table)
-
-
-def fold_kernel(count_ref, wide_ref, out_ref):
+    wide[...] = (mm(low, hot) + mm(middle, hot)) + mm(high, hot)
+    pl.semaphore_wait(pltpu.get_barrier_semaphore(), len(AROUND))
+    copies = [to_column(o, wide, held, send_sem, recv_sem) for o in AROUND]
+    for copy in copies:
+        copy.start()
+    axis = lax.broadcasted_iota(jnp.int32, (4, width), 0)
+    table_ref[16:20, :] = wide[...]
+    for copy in copies:
+        copy.wait()
+    for o in AROUND:
+        shift = jnp.where(
+            axis == 0,
+            col_width * (o // 3 - 1),
+            jnp.where(axis == 1, col_width * (o % 3 - 1), 0.0),
+        )
+        table_ref[4 * o : 4 * o + 4, :] = held[o] + shift
+
+
+def fold_kernel(count_ref, wide_ref, out_ref, sent, held, send_sem, recv_sem):
+    greet()
     width = wide_ref.shape[1]
     slots = out_ref.shape[1]
+    blank = jnp.zeros((1, width), F32)
+    for o in AROUND:
+        sent[o] = jnp.concatenate([wide_ref[3 * o : 3 * o + 3, :], blank], axis=0)
+    pl.semaphore_wait(pltpu.get_barrier_semaphore(), len(AROUND))
+    copies = [to_column(o, sent.at[o], held, send_sem, recv_sem) for o in AROUND]
+    for copy in copies:
+        copy.start()
     count = count_ref[0, 0].astype(F32)
     hot = (
         wrapped_index((width, slots), 0, count)
         == lax.broadcasted_iota(jnp.int32, (width, slots), 1).astype(F32)
     )
-    table = jnp.where(hot, 1.0, 0.0).astype(BF16)
-    high, middle, low = split(wide_ref[...], 3)
-    out_ref[...] = (mm(low, table) + mm(middle, table)) + mm(high, table)
+    hot = jnp.where(hot, 1.0, 0.0).astype(BF16)
+    total = jnp.concatenate([wide_ref[12:15, :], blank], axis=0)
+    for copy in copies:
+        copy.wait()
+    for o in AROUND:
+        total = total + held[o]
+    high, middle, low = split(total, 3)
+    out_ref[...] = ((mm(low, hot) + mm(middle, hot)) + mm(high, hot))[:3]
 
 
 def codes_of(index):
@@ -232,7 +291,7 @@
                 jnp.where(order == 2, 1.0 - partner, jnp.where(order == 3, partner, 0.0)),
             ),
         )
-        inputs = jnp.concatenate([bessel, one_hot], axis=0).astype(BF16)
+        inputs = jnp.concatenate([bessel, one_hot[:4]], axis=0).astype(BF16)
         hidden, slope_h = silu_pair(mm(embed_ref[...], inputs))
         hidden_d[c] = slope_h.astype(BF16)
         active, slope_m = silu_pair(mm(mixer_ref[...], hidden.astype(BF16)))
@@ -323,11 +382,6 @@
     wide_ref[:, pl.ds(start, width)] += total
 
 
-def shifted(value, axis, by):
-    peers = lax.axis_size(axis)
-    return lax.ppermute(value, axis, [(i, (i + by) % peers) for i in range(peers)])
-
-
 def body(
     positions,
     species,
@@ -349,39 +403,29 @@
     column = jnp.concatenate(
         [positions.reshape(3, slots), species.reshape(1, slots).astype(F32)], axis=0
     )
-    wide = pl.pallas_call(
+    sems = [pltpu.SemaphoreType.DMA((9,)), pltpu.SemaphoreType.DMA((9,))]
+    table = pl.pallas_call(
         spread_kernel,
-        out_shape=jax.ShapeDtypeStruct((4, width), F32),
+        out_shape=jax.ShapeDtypeStruct((36, width), F32),
         in_specs=[smem, vmem],
         out_specs=vmem,
-        compiler_params=params,
+        scratch_shapes=[pltpu.VMEM((4, width), F32), pltpu.VMEM((9, 4, width), F32)] + sems,
+        compiler_params=pltpu.CompilerParams(
+            vmem_limit_bytes=VMEM_LIMIT, collective_id=0, has_side_effects=True
+        ),
     )(counts, column)
-    beside = jnp.stack([shifted(wide, "gx", 1), wide, shifted(wide, "gx", -1)])
-    around = jnp.stack([shifted(beside, "gy", 1), beside, shifted(beside, "gy", -1)], axis=1)
-    steps = jnp.arange(3, dtype=F32) - 1.0
-    shift = jnp.stack(
-        [
-            jnp.broadcast_to(col_width * steps[:, None], (3, 3)),
-            jnp.broadcast_to(col_width * steps[None, :], (3, 3)),
-            jnp.zeros((3, 3), F32),
-            jnp.zeros((3, 3), F32),
-        ],
-        axis=2,
-    )
-    table = (around + shift[..., None]).reshape(36, width)
 
     chunks = neigh // ROWS
     span = ROWS * LANES
     latent = mixer_weight.shape[0]
-    embed = jnp.pad(embed_weight, ((0, 0), (0, 4)))
     whole = lambda array: pl.BlockSpec(array.shape, lambda b: (0,) * array.ndim)
     by_block = lambda rows: pl.BlockSpec((rows, LANES), lambda b: (0, b))
     operands = [
-        embed,
+        embed_weight,
         mixer_weight,
         tensor_weight,
         update_weight,
-        embed.T,
+        embed_weight.T,
         mixer_weight.T,
         tensor_weight.T,
         update_weight.T,
@@ -415,16 +459,16 @@
         compiler_params=params,
     )(counts, pair_scale, table, column, neighbours.reshape(neigh, slots), *operands)
 
-    partials = partials.reshape(3, 3, 3, width)
-    line = partials[1] + shifted(partials[0], "gx", -1) + shifted(partials[2], "gx", 1)
-    centre = line[1] + shifted(line[0], "gy", -1) + shifted(line[2], "gy", 1)
     forces = pl.pallas_call(
         fold_kernel,
         out_shape=jax.ShapeDtypeStruct((3, slots), F32),
         in_specs=[smem, vmem],
         out_specs=vmem,
-        compiler_params=params,
-    )(counts, centre)
+        scratch_shapes=[pltpu.VMEM((9, 4, width), F32), pltpu.VMEM((9, 4, width), F32)] + sems,
+        compiler_params=pltpu.CompilerParams(
+            vmem_limit_bytes=VMEM_LIMIT, collective_id=1, has_side_effects=True
+        ),
+    )(counts, partials)
     return energy.reshape(1, 1, slots), forces.reshape(3, 1, 1, slots)
 
 

time: 89.7 us -> 80.5 us (0.90)
  Pallas kernels: 59.1 us -> 75 us
  starting transfers between devices: 11.9 us -> 0 us
  waiting for transfers between devices: 11.2 us -> 0 us
  local copies, waits for them, and re-layouts: 4.8 us -> 3.07 us
    ppermute x8 -> x0, starting transfers between devices: 11.9 us -> none  [shifted(): lax.ppermute(value, axis, [(i, (i + by) % peers) for i in range(peers)])]
    ppermute x8 -> x0, waiting for transfers between devices: 11.2 us -> none  [shifted(): lax.ppermute(value, axis, [(i, (i + by) % peers) for i in range(peers)])]
    pallas_call x1, Pallas kernels: 0.39 us -> 9.08 us  [body(): pl.pallas_call(spread_kernel, out_shape=jax.ShapeDtypeStruct((36, width),...]
    pallas_call x1, Pallas kernels: 0.46 us -> 7.8 us  [body(): pl.pallas_call(fold_kernel, out_shape=jax.ShapeDtypeStruct((3, slots), F3...]
    unnamed x21 -> x23, local copies, waits for them, and re-layouts: 4.28 us -> 2.97 us
  transfers between devices with their start and end apart: 8 -> 0, of which waited for: 6 -> 0; matrix products, arithmetic and copies ran while one was open for 1% -> 0% of each run, Pallas kernels for 0% -> 0%
where the time goes in v1:
time: 80.5 us; the launch traced here: 80.1 us
  Pallas kernels  75 us (93%)
  local copies, waits for them, and re-layouts  3.07 us (4%)
  between operations  1.41 us (2%)
    pallas_call x1, Pallas kernels, body(): pl.pallas_call(layer_kernel, grid=(slots // LANES,), out_shape=(jax.Shape...  58.1 us
    pallas_call x1, Pallas kernels, body(): pl.pallas_call(spread_kernel, out_shape=jax.ShapeDtypeStruct((36, width),...  9.08 us
    pallas_call x1, Pallas kernels, body(): pl.pallas_call(fold_kernel, out_shape=jax.ShapeDtypeStruct((3, slots), F3...  7.8 us
    unnamed x23, local copies, waits for them, and re-layouts  2.97 us

profile of v1, /device:TPU:0, one launch (start us, length us, event | category | flops | bytes accessed | tf_op | source)
XLA Modules:
  0.0 80.1 jit_solution(4388577972894435368)
XLA Ops:
  0.6 0.0 copy-start.6
  1.3 0.7 convert_bitcast_fusion
  2.0 0.0 copy-done.6
  2.0 0.0 copy-start.3
  2.0 0.0 copy-start
  2.0 0.7 copy-done.3
  2.7 0.1 copy.15.embed_ref
  2.8 0.0 copy-done
  2.8 0.0 copy-start.2
  2.8 0.0 copy-start.7
  2.8 0.1 copy.12
  2.9 0.0 copy-start.1
  2.9 0.0 copy-start.5
  2.9 0.6 copy-done.2
  3.5 0.1 copy.13
  3.6 0.0 copy-done.1
  3.6 0.1 copy.14
  3.7 0.0 copy-done.7
  3.7 0.1 copy.16.output_ref
  3.8 9.1 %shard_map.113.table_ref = f32[36,640]{1,0:T(8,128)S(1)} custom-call(s32[1,1]{1,0:T(1,128)S(6)} %copy.24.count_ref, f32[4,512]{1,0:T(4,128)S(1)} %pad_maximum_fusion.column_ref.own_ref), custom_call_target="tpu_custom_call" | custom-call | tf_op jit(solution)/shard_map/pallas_call | solution.py:407
  12.9 0.0 copy-done.5
  13.0 0.0 copy-start.4
  13.0 0.7 copy-done.4
  13.6 58.1 %shard_map.114 = (f32[1,512]{1,0:T(1,128)}, f32[27,640]{1,0:T(8,128)S(1)}) custom-call(s32[1,1]{1,0:T(1,128)S(6)} %copy.24.count_ref, f32[2,2]{1,0:T(2,128)S(1)} %copy-done.4, f32[36,640]{1,0:T(8,128)S(1)} %shard_map.113.table_ref, f32[4,512]{1,0:T(4,128)S(1)} %pad_maximum_fusion.column_ref.own_ref, s32[64,512]{1,0:T(8,128)S(1)} %bitcast.15, ...), custom_call_target="tpu_custom_call" | custom-call | tf_op jit(solution)/shard_map/pallas_call | solution.py:434
  71.7 7.8 %shard_map.115 = f32[3,512]{1,0:T(4,128)S(1)} custom-call(s32[1,1]{1,0:T(1,128)S(6)} %copy.24.count_ref, f32[27,640]{1,0:T(8,128)S(1)} %get-tuple-element.5.wide_ref), custom_call_target="tpu_custom_call" | custom-call | tf_op jit(solution)/shard_map/pallas_call | solution.py:462
  79.5 0.6 copy.17
  (3 shorter events, 0.0 us)
Async XLA Ops:
  0.6 1.4 %copy-start.6 = (f32[3,1,1,512]{3,2,1,0:T(1,128)S(1)}, f32[3,1,1,512]{3,2,1,0:T(1,128)}, u32[]{:S(2)}) copy-start(f32[3,1,1,512]{3,2,1,0:T(1,128)} %param.10) | copy-start | bytes 18436
  2.0 0.7 copy-start.3
  2.0 0.8 copy-start
  2.8 0.7 copy-start.2
  2.8 0.9 %copy-start.7 = (f32[64]{0:T(128)S(1)}, f32[64]{0:T(128)}, u32[]{:S(2)}) copy-start(f32[64]{0:T(128)} %param.18) | copy-start | bytes 772
  2.9 0.7 copy-start.1
  2.9 10.0 %copy-start.5 = (s32[64,1,1,512]{3,2,1,0:T(1,128)S(1)}, s32[64,1,1,512]{3,2,1,0:T(1,128)}, u32[]{:S(2)}) copy-start(s32[64,1,1,512]{3,2,1,0:T(1,128)} %param.13) | copy-start | bytes 393220
  13.0 0.7 copy-start.4

commit v2 on v1

--- a/solution.py
+++ b/solution.py
@@ -152,6 +152,7 @@
 
 
 def silu_pair(x):
+    x = x.astype(BF16)
     sig = 0.5 * jnp.tanh(0.5 * x) + 0.5
     s = x * sig
     return s, sig + s - s * sig
@@ -293,11 +294,12 @@
         )
         inputs = jnp.concatenate([bessel, one_hot[:4]], axis=0).astype(BF16)
         hidden, slope_h = silu_pair(mm(embed_ref[...], inputs))
-        hidden_d[c] = slope_h.astype(BF16)
-        active, slope_m = silu_pair(mm(mixer_ref[...], hidden.astype(BF16)))
-        mixed[c] = active.astype(BF16)
-        mixed_d[c] = (slope_m * envelope).astype(BF16)
-        lat = (active * envelope).astype(BF16)
+        hidden_d[c] = slope_h
+        active, slope_m = silu_pair(mm(mixer_ref[...], hidden))
+        envelope = jnp.broadcast_to(envelope, active.shape).astype(BF16)
+        mixed[c] = active
+        mixed_d[c] = slope_m * envelope
+        lat = active * envelope
         latent[c] = lat
         t = mm(tensor_ref[...], lat)
         tensor[c] = t
@@ -307,7 +309,7 @@
             environment[m + 1] += lane_sum(env_w * row(which, c))
         return carry
 
-    lax.fori_loop(0, chunks, first, 0)
+    lax.fori_loop(0, chunks, first, 0, unroll=8)
 
     def second(c, carry):
         weight = row(WEIGHT, c)
@@ -321,11 +323,11 @@
         joined = jnp.concatenate([lat, scalars], axis=0)
         s, slope = silu_pair(mm(update_ref[...], joined))
         out = output_ref[...]
-        value = column_sum(out * (lat.astype(F32) + s))
+        value = column_sum(out * (lat.astype(F32) + s.astype(F32)))
         energy_ref[...] += lane_sum(value * weight)
         put(D_ENV, c, value * row(SCALE, c))
         seed = out * weight
-        back = mm(update_t_ref[...], (seed * slope).astype(BF16))
+        back = mm(update_t_ref[...], seed.astype(BF16) * slope)
         latent_g[c] = (seed + back[:64]).astype(BF16)
         even_g, odd_g = 0.25 * back[64:80], 0.25 * back[80:96]
         feature_g[c] = (even_g * envs[0] + odd_g * mixed_env).astype(BF16)
@@ -336,7 +338,7 @@
             put(D_HX + m, c, column_sum(odd * envs[m + 1]))
         return carry
 
-    lax.fori_loop(0, chunks, second, 0)
+    lax.fori_loop(0, chunks, second, 0, unroll=8)
 
     def third(c, carry):
         harm = [row(which, c) for which in (HX, HY, HZ)]
@@ -347,16 +349,16 @@
         total = latent_g[c].astype(F32) + mm(tensor_t_ref[...], tensor_g)
         at = pl.ds(pl.multiple_of(c * ROWS, ROWS), ROWS)
         dplane[D_ENV, at, :] += tile_of(column_sum(total * mixed[c].astype(F32)))
-        mixed_g = (total * mixed_d[c].astype(F32)).astype(BF16)
+        mixed_g = total.astype(BF16) * mixed_d[c]
         hidden_g = mm(mixer_t_ref[...], mixed_g)
-        hidden_g = (hidden_g * hidden_d[c].astype(F32)).astype(BF16)
+        hidden_g = hidden_g.astype(BF16) * hidden_d[c]
         bessel_g = mm(embed_t_ref[...], hidden_g)[:8]
         put(D_DIST, c, column_sum(bessel_g * bessel_d[c]))
         for m in range(3):
             dplane[D_HX + m, at, :] += tile_of(column_sum(env_w * grads[m + 1]))
         return carry
 
-    lax.fori_loop(0, chunks, third, 0)
+    lax.fori_loop(0, chunks, third, 0, unroll=8)
 
     hx, hy, hz = plane[HX], plane[HY], plane[HZ]
     gx, gy, gz = dplane[D_HX], dplane[D_HY], dplane[D_HZ]

time: 80.5 us -> 64.5 us (0.80)
  Pallas kernels: 75 us -> 59 us
    pallas_call x1, Pallas kernels: 58.1 us -> 42.1 us  [body(): pl.pallas_call(layer_kernel, grid=(slots // LANES,), out_shape=(jax.Shape...]
where the time goes in v2:
time: 64.5 us; the launch traced here: 64.2 us
  Pallas kernels  59 us (91%)
  local copies, waits for them, and re-layouts  3.07 us (5%)
  between operations  1.41 us (2%)
  other arithmetic  0.69 us (1%)
    pallas_call x1, Pallas kernels, body(): pl.pallas_call(layer_kernel, grid=(slots // LANES,), out_shape=(jax.Shape...  42.1 us
    pallas_call x1, Pallas kernels, body(): pl.pallas_call(spread_kernel, out_shape=jax.ShapeDtypeStruct((36, width),...  9.08 us
    pallas_call x1, Pallas kernels, body(): pl.pallas_call(fold_kernel, out_shape=jax.ShapeDtypeStruct((3, slots), F3...  7.81 us
    unnamed x23, local copies, waits for them, and re-layouts  2.97 us

profile of v2, /device:TPU:0, one launch (start us, length us, event | category | flops | bytes accessed | tf_op | source)
XLA Modules:
  0.0 64.2 jit_solution(10595280937524889009)
XLA Ops:
  0.6 0.0 copy-start.6
  1.3 0.7 %convert_bitcast_fusion = f32[1,512]{1,0:T(1,128)S(1)} fusion(s32[1,1,512]{2,1,0:T(1,128)} %param.11), kind=kLoop, calls=%fused_computation.3 | loop fusion | flops 512 | bytes 4096 | tf_op jit(solution)/shard_map/convert_element_type | solution.py:406
  2.0 0.0 copy-done.6
  2.0 0.0 copy-start.3
  2.0 0.0 copy-start
  2.0 0.7 %copy-done.3 = bf16[64,12]{0,1:T(8,128)(2,1)S(1)} copy-done((bf16[64,12]{0,1:T(8,128)(2,1)S(1)}, bf16[64,12]{0,1:T(8,128)(2,1)}, u32[]{:S(2)}) %copy-start.3) | copy-done | bytes 1560
  2.7 0.1 copy.15.embed_ref
  2.8 0.0 copy-done
  2.8 0.0 copy-start.2
  2.8 0.0 copy-start.7
  2.8 0.1 copy.12
  2.9 0.0 copy-start.1
  2.9 0.0 copy-start.5
  2.9 0.6 copy-done.2
  3.5 0.1 copy.13
  3.6 0.0 copy-done.1
  3.6 0.1 copy.14
  3.7 0.0 copy-done.7
  3.7 0.1 copy.16.output_ref
  3.8 9.1 %shard_map.113.table_ref = f32[36,640]{1,0:T(8,128)S(1)} custom-call(s32[1,1]{1,0:T(1,128)S(6)} %copy.24.count_ref, f32[4,512]{1,0:T(4,128)S(1)} %pad_maximum_fusion.column_ref.own_ref), custom_call_target="tpu_custom_call" | custom-call | tf_op jit(solution)/shard_map/pallas_call | solution.py:409
  12.9 0.0 copy-done.5
  13.0 0.0 copy-start.4
  13.0 0.7 %copy-done.4 = f32[2,2]{1,0:T(2,128)S(1)} copy-done((f32[2,2]{1,0:T(2,128)S(1)}, f32[2,2]{1,0:T(2,128)}, u32[]{:S(2)}) %copy-start.4) | copy-done | bytes 40
  13.6 42.1 %shard_map.114 = (f32[1,512]{1,0:T(1,128)}, f32[27,640]{1,0:T(8,128)S(1)}) custom-call(s32[1,1]{1,0:T(1,128)S(6)} %copy.24.count_ref, f32[2,2]{1,0:T(2,128)S(1)} %copy-done.4, f32[36,640]{1,0:T(8,128)S(1)} %shard_map.113.table_ref, f32[4,512]{1,0:T(4,128)S(1)} %pad_maximum_fusion.column_ref.own_ref, s32[64,512]{1,0:T(8,128)S(1)} %bitcast.15, ...), custom_call_target="tpu_custom_call" | custom-call | tf_op jit(solution)/shard_map/pallas_call | solution.py:436
  55.8 7.8 %shard_map.115 = f32[3,512]{1,0:T(4,128)S(1)} custom-call(s32[1,1]{1,0:T(1,128)S(6)} %copy.24.count_ref, f32[27,640]{1,0:T(8,128)S(1)} %get-tuple-element.5.wide_ref), custom_call_target="tpu_custom_call" | custom-call | tf_op jit(solution)/shard_map/pallas_call | solution.py:464
  63.6 0.6 copy.17
  (3 shorter events, 0.0 us)
Async XLA Ops:
  0.6 1.4 %copy-start.6 = (f32[3,1,1,512]{3,2,1,0:T(1,128)S(1)}, f32[3,1,1,512]{3,2,1,0:T(1,128)}, u32[]{:S(2)}) copy-start(f32[3,1,1,512]{3,2,1,0:T(1,128)} %param.10) | copy-start | bytes 18436
  2.0 0.7 %copy-start.3 = (bf16[64,12]{0,1:T(8,128)(2,1)S(1)}, bf16[64,12]{0,1:T(8,128)(2,1)}, u32[]{:S(2)}) copy-start(bf16[64,12]{0,1:T(8,128)(2,1)} %param.14) | copy-start | bytes 4612
  2.0 0.8 %copy-start = (bf16[64,64]{1,0:T(8,128)(2,1)S(1)}, bf16[64,64]{1,0:T(8,128)(2,1)}, u32[]{:S(2)}) copy-start(bf16[64,64]{1,0:T(8,128)(2,1)} %mixer_ref.1) | copy-start | bytes 24580
  2.8 0.7 %copy-start.2 = (bf16[32,64]{1,0:T(8,128)(2,1)S(1)}, bf16[32,64]{1,0:T(8,128)(2,1)}, u32[]{:S(2)}) copy-start(bf16[32,64]{1,0:T(8,128)(2,1)} %tensor_ref.1) | copy-start | bytes 12292
  2.8 0.9 %copy-start.7 = (f32[64]{0:T(128)S(1)}, f32[64]{0:T(128)}, u32[]{:S(2)}) copy-start(f32[64]{0:T(128)} %param.18) | copy-start | bytes 772
  2.9 0.7 %copy-start.1 = (bf16[64,96]{1,0:T(8,128)(2,1)S(1)}, bf16[64,96]{1,0:T(8,128)(2,1)}, u32[]{:S(2)}) copy-start(bf16[64,96]{1,0:T(8,128)(2,1)} %update_ref.1) | copy-start | bytes 36868
  2.9 10.0 %copy-start.5 = (s32[64,1,1,512]{3,2,1,0:T(1,128)S(1)}, s32[64,1,1,512]{3,2,1,0:T(1,128)}, u32[]{:S(2)}) copy-start(s32[64,1,1,512]{3,2,1,0:T(1,128)} %param.13) | copy-start | bytes 393220
  13.0 0.7 %copy-start.4 = (f32[2,2]{1,0:T(2,128)S(1)}, f32[2,2]{1,0:T(2,128)}, u32[]{:S(2)}) copy-start(f32[2,2]{1,0:T(2,128)} %scale_ref.1) | copy-start | bytes 52

commit v3 on v2

--- a/solution.py
+++ b/solution.py
@@ -179,14 +179,10 @@
     table_ref,
     own_ref,
     codes_ref,
-    embed_ref,
+    embed_t_ref,
     mixer_ref,
     tensor_ref,
     update_ref,
-    embed_t_ref,
-    mixer_t_ref,
-    tensor_t_ref,
-    update_t_ref,
     output_ref,
     energy_ref,
     wide_ref,
@@ -203,6 +199,10 @@
     environment,
     environment_g,
     per_stride,
+    embed_ref,
+    mixer_t_ref,
+    tensor_t_ref,
+    update_t_ref,
 ):
     block = pl.program_id(0)
     neigh = codes_ref.shape[0]
@@ -214,6 +214,10 @@
     def _():
         wide_ref[...] = jnp.zeros_like(wide_ref)
         per_stride[...] = jnp.zeros_like(per_stride)
+        embed_ref[...] = embed_t_ref[...].astype(F32).T.astype(BF16)
+        mixer_t_ref[...] = mixer_ref[...].astype(F32).T.astype(BF16)
+        tensor_t_ref[...] = tensor_ref[...].astype(F32).T.astype(BF16)
+        update_t_ref[...] = update_ref[...].astype(F32).T.astype(BF16)
 
     start = pl.multiple_of(block * LANES, LANES)
     slab = table_ref[:, pl.ds(start, width)]
@@ -423,14 +427,10 @@
     whole = lambda array: pl.BlockSpec(array.shape, lambda b: (0,) * array.ndim)
     by_block = lambda rows: pl.BlockSpec((rows, LANES), lambda b: (0, b))
     operands = [
-        embed_weight,
+        embed_weight.T,
         mixer_weight,
         tensor_weight,
         update_weight,
-        embed_weight.T,
-        mixer_weight.T,
-        tensor_weight.T,
-        update_weight.T,
         output_weight.reshape(latent, 1),
     ]
     energy, partials = pl.pallas_call(
@@ -457,6 +457,10 @@
             pltpu.VMEM((4, 16, LANES), F32),
             pltpu.VMEM((4, 16, LANES), F32),
             pltpu.VMEM((STRIDES, 27, LANES), F32),
+            pltpu.VMEM(embed_weight.shape, BF16),
+            pltpu.VMEM(mixer_weight.shape[::-1], BF16),
+            pltpu.VMEM(tensor_weight.shape[::-1], BF16),
+            pltpu.VMEM(update_weight.shape[::-1], BF16),
         ],
         compiler_params=params,
     )(counts, pair_scale, table, column, neighbours.reshape(neigh, slots), *operands)

time: 64.5 us -> 64.4 us (level)
    unnamed x23 -> x15, local copies, waits for them, and re-layouts: 2.97 us -> 2 us
    reshape x1, local copies, waits for them, and re-layouts: 0.1 us -> 0.75 us  [body(): output_weight.reshape(latent, 1)]
where the time goes in v3:
time: 64.4 us; the launch traced here: 64 us
  Pallas kernels  59.2 us (92%)
  local copies, waits for them, and re-layouts  2.75 us (4%)
  between operations  1.4 us (2%)
  other arithmetic  0.7 us (1%)
    pallas_call x1, Pallas kernels, body(): pl.pallas_call(layer_kernel, grid=(slots // LANES,), out_shape=(jax.Shape...  42.3 us
    pallas_call x1, Pallas kernels, body(): pl.pallas_call(spread_kernel, out_shape=jax.ShapeDtypeStruct((36, width),...  9.08 us
    pallas_call x1, Pallas kernels, body(): pl.pallas_call(fold_kernel, out_shape=jax.ShapeDtypeStruct((3, slots), F3...  7.82 us
    unnamed x15, local copies, waits for them, and re-layouts  2 us

profile of v3, /device:TPU:0, one launch (start us, length us, event | category | flops | bytes accessed | tf_op | source)
XLA Modules:
  0.0 64.0 jit_solution(4746350580442610070)
XLA Ops:
  0.6 0.0 copy-start.5
  1.3 0.7 %convert_bitcast_fusion = f32[1,512]{1,0:T(1,128)S(1)} fusion(s32[1,1,512]{2,1,0:T(1,128)} %param.11), kind=kLoop, calls=%fused_computation.3 | loop fusion | flops 512 | bytes 4096 | tf_op jit(solution)/shard_map/convert_element_type | solution.py:410
  2.0 0.7 %copy.19 = f32[3,1,1,512]{3,0,1,2:T(4,128)S(1)} copy(f32[3,1,1,512]{3,2,1,0:T(1,128)} %param.10) | data formatting | bytes 12288
  2.7 0.7 %copy.12.output_ref = f32[64,1]{1,0:T(8,128)S(1)} copy(f32[64,1]{0,1:T(1,128)} %bitcast.16) | data formatting | bytes 512 | tf_op jit(solution)/shard_map/reshape | solution.py:434
  3.5 9.1 %shard_map.113.table_ref = f32[36,640]{1,0:T(8,128)S(1)} custom-call(s32[1,1]{1,0:T(1,128)S(6)} %copy.20.count_ref, f32[4,512]{1,0:T(4,128)S(1)} %pad_maximum_fusion.column_ref.own_ref), custom_call_target="tpu_custom_call" | custom-call | tf_op jit(solution)/shard_map/pallas_call | solution.py:413
  12.5 0.0 copy-done.5
  12.6 0.0 copy-start
  12.6 0.0 copy-start.1
  12.6 0.0 copy-start.2
  12.6 0.0 copy-start.3
  12.6 0.0 copy-start.4
  12.6 0.6 %copy-done = bf16[64,64]{1,0:T(8,128)(2,1)S(1)} copy-done((bf16[64,64]{1,0:T(8,128)(2,1)S(1)}, bf16[64,64]{1,0:T(8,128)(2,1)}, u32[]{:S(2)}) %copy-start) | copy-done | bytes 8216
  13.3 0.0 copy-done.1
  13.3 0.0 copy-done.2
  13.3 0.0 copy-done.3
  13.3 0.0 copy-done.4
  13.3 42.3 %shard_map.114 = (f32[1,512]{1,0:T(1,128)}, f32[27,640]{1,0:T(8,128)S(1)}) custom-call(s32[1,1]{1,0:T(1,128)S(6)} %copy.20.count_ref, f32[2,2]{1,0:T(2,128)S(1)} %copy-done.4, f32[36,640]{1,0:T(8,128)S(1)} %shard_map.113.table_ref, f32[4,512]{1,0:T(4,128)S(1)} %pad_maximum_fusion.column_ref.own_ref, s32[64,512]{1,0:T(8,128)S(1)} %bitcast.12, ...), custom_call_target="tpu_custom_call" | custom-call | tf_op jit(solution)/shard_map/pallas_call | solution.py:436
  55.6 7.8 %shard_map.115 = f32[3,512]{1,0:T(4,128)S(1)} custom-call(s32[1,1]{1,0:T(1,128)S(6)} %copy.20.count_ref, f32[27,640]{1,0:T(8,128)S(1)} %get-tuple-element.5.wide_ref), custom_call_target="tpu_custom_call" | custom-call | tf_op jit(solution)/shard_map/pallas_call | solution.py:468
  63.4 0.6 copy.13
  (2 shorter events, 0.0 us)
Async XLA Ops:
  0.6 11.9 %copy-start.5 = (s32[64,1,1,512]{3,2,1,0:T(1,128)S(1)}, s32[64,1,1,512]{3,2,1,0:T(1,128)}, u32[]{:S(2)}) copy-start(s32[64,1,1,512]{3,2,1,0:T(1,128)} %param.13) | copy-start | bytes 393220
  12.6 0.7 %copy-start = (bf16[64,64]{1,0:T(8,128)(2,1)S(1)}, bf16[64,64]{1,0:T(8,128)(2,1)}, u32[]{:S(2)}) copy-start(bf16[64,64]{1,0:T(8,128)(2,1)} %mixer_ref.1) | copy-start | bytes 24580
  12.6 0.7 %copy-start.1 = (bf16[64,96]{1,0:T(8,128)(2,1)S(1)}, bf16[64,96]{1,0:T(8,128)(2,1)}, u32[]{:S(2)}) copy-start(bf16[64,96]{1,0:T(8,128)(2,1)} %update_ref.1) | copy-start | bytes 36868
  12.6 0.7 %copy-start.2 = (bf16[32,64]{1,0:T(8,128)(2,1)S(1)}, bf16[32,64]{1,0:T(8,128)(2,1)}, u32[]{:S(2)}) copy-start(bf16[32,64]{1,0:T(8,128)(2,1)} %tensor_ref.1) | copy-start | bytes 12292
  12.6 0.7 %copy-start.3 = (bf16[64,12]{0,1:T(8,128)(2,1)S(1)}, bf16[64,12]{0,1:T(8,128)(2,1)}, u32[]{:S(2)}) copy-start(bf16[64,12]{0,1:T(8,128)(2,1)} %param.14) | copy-start | bytes 4612
  12.6 0.7 %copy-start.4 = (f32[2,2]{1,0:T(2,128)S(1)}, f32[2,2]{1,0:T(2,128)}, u32[]{:S(2)}) copy-start(f32[2,2]{1,0:T(2,128)} %scale_ref.1) | copy-start | bytes 52
